TPU v7x, 256 devices: a whole 4x4x8 slice. The times are simulated.
256 devices in a mesh: section: 8 (over z_hi, x), expert: 32 (over z_lo, y, core).
Axes of the slice: x: 4, y: 4, z: 8 (z_hi: 2, z_lo: 4; z = z_hi * 4 + z_lo), core: 2. Of those that a mesh axis runs over, the one named last changes fastest.
Arguments:
- x_a: bfloat16 [32768, 7168], P(('section', 'expert')), may hold values from -6 to 6
- routes_a: int32 [32768], P(('section', 'expert')), may hold values from 0 to 4, as said below
- scale_a: float32 [32768], P(('section', 'expert')), may hold values from 0.1 to 1
- cotangent_b: bfloat16 [32768, 7168], P(('section', 'expert')), may hold values from -6 to 6
- routes_b: int32 [32768], P(('section', 'expert')), may hold values from 0 to 4, as said below
- scale_b: float32 [32768], P(('section', 'expert')), may hold values from 0.1 to 1
- saved_b: bfloat16 [32768, 2048], P(('section', 'expert')), may hold values from -6 to 6
- w_gate_up: bfloat16 [229376, 2048], P(('section', 'expert')), may hold values from -0.0625 to 0.0625
- w_down_t: bfloat16 [229376, 1024], P(('section', 'expert')), may hold values from -0.1875 to 0.1875
Outputs:
- handoff: bfloat16 [32768, 7168], P(('section', 'expert'))
- grad_handoff: bfloat16 [32768, 7168], P(('section', 'expert'))
Inputs may be any that keep to these rules, and one draw needn't show every extreme that they name: `routes_a`: 4 means that the token's route leads to an expert outside this window. Among the 128 tokens of one device no value below 4 occurs more than 12 times, and in every draw some value occurs exactly 12 times on every device. `routes_b`: as routes_a.
All inputs are finite; a program needn't handle non-finite values.
Results may differ from a plain program's by a relative error of at most 0.002.
Values may be sent and summed in bfloat16 or wider, within the bound.
A program may use at most 128 MiB of HBM per device.

v0:
```python
import jax
import jax.numpy as jnp
from jax import lax
from jax.sharding import PartitionSpec as P

FF = 1024
GROUP = 8
CAP = 12


def swapped(block, axis, apart):
    count = lax.axis_size(axis)
    route = []
    for low in range(count):
        high = low | 1 << apart
        if high != low and high < count:
            route += [(low, high), (high, low)]
    return lax.ppermute(block, axis, route)


def passed_along(value, axis, steps):
    count = lax.axis_size(axis)
    pairs = [(source, (source + steps) % count) for source in range(count)]
    return lax.ppermute(value, axis, pairs)


def slot_table(routes, experts):
    expert_ids = jnp.arange(experts, dtype=jnp.int32)
    matches = (routes[None, :] == expert_ids[:, None]).astype(jnp.int32)
    ranking = jnp.cumsum(matches, axis=1) - 1
    slot_ids = jnp.arange(CAP, dtype=jnp.int32)
    placed = (matches[:, None, :] == 1) & (ranking[:, None, :] == slot_ids[None, :, None])
    return placed.astype(jnp.bfloat16)


def whole_sum(partial_value):
    for bit_index in range(GROUP.bit_length() - 1):
        partial_value = partial_value + swapped(partial_value, "expert", bit_index)
    return partial_value


def silu_grads(dhidden, saved_rows):
    pre_gate = saved_rows[:, 0].astype(jnp.float32)
    pre_up = saved_rows[:, 1].astype(jnp.float32)
    sigmoid_gate = jax.nn.sigmoid(pre_gate)
    grad_gate = dhidden * pre_up * sigmoid_gate * (1.0 + pre_gate * (1.0 - sigmoid_gate))
    grad_up = dhidden * pre_gate * sigmoid_gate
    return jnp.stack([grad_gate, grad_up], axis=1).astype(jnp.bfloat16)


def per_device(
    x_a, routes_a, scale_a, cotangent_b, routes_b, scale_b, saved_b, w_gate_up, w_down_t
):
    experts = lax.axis_size("expert") // GROUP
    tok_rows = x_a.shape[0]
    model_width = x_a.shape[1]
    slice_width = model_width // GROUP
    table_fwd = slot_table(routes_a, experts)
    token_slices = x_a.reshape(tok_rows, GROUP, slice_width)
    outbound = jnp.einsum(
        "ect,tkd->ekcd", table_fwd, token_slices, preferred_element_type=jnp.float32
    ).astype(jnp.bfloat16)
    arrived = lax.all_to_all(
        outbound.reshape(-1, slice_width), "expert", split_axis=0, concat_axis=0, tiled=True
    )
    projected = jnp.dot(arrived, w_gate_up, preferred_element_type=jnp.float32)
    slot_count = projected.shape[0]
    summed = whole_sum(projected).reshape(slot_count, 2, FF)
    hidden = (jax.nn.silu(summed[:, 0]) * summed[:, 1]).astype(jnp.bfloat16)
    expert_out = jnp.einsum(
        "rf,df->rd", hidden, w_down_t, preferred_element_type=jnp.float32
    ).astype(jnp.bfloat16)
    returned = lax.all_to_all(
        expert_out, "expert", split_axis=0, concat_axis=0, tiled=True
    ).reshape(experts, GROUP, CAP, slice_width)
    combined = jnp.einsum(
        "ect,ekcd->tkd", table_fwd, returned, preferred_element_type=jnp.float32
    ).reshape(tok_rows, model_width)
    forward_out = (x_a.astype(jnp.float32) + scale_a[:, None] * combined).astype(jnp.bfloat16)
    handoff = passed_along(forward_out, "section", 1)
    table_bwd = slot_table(routes_b, experts)
    scaled = (scale_b[:, None] * cotangent_b.astype(jnp.float32)).astype(jnp.bfloat16)
    grad_out = (
        jnp.einsum(
            "ect,tkd->ekcd",
            table_bwd,
            scaled.reshape(tok_rows, GROUP, slice_width),
            preferred_element_type=jnp.float32,
        )
        .astype(jnp.bfloat16)
        .reshape(-1, slice_width)
    )
    picked = jnp.einsum(
        "ect,tf->ecf", table_bwd, saved_b, preferred_element_type=jnp.float32
    ).astype(jnp.bfloat16)
    saved_out = jnp.broadcast_to(picked[:, None], (experts, GROUP, CAP, 2 * FF)).reshape(-1, 2 * FF)
    grad_in, saved_in = (
        lax.all_to_all(grad_out, "expert", split_axis=0, concat_axis=0, tiled=True),
        lax.all_to_all(saved_out, "expert", split_axis=0, concat_axis=0, tiled=True),
    )
    dhidden = jnp.einsum("rd,df->rf", grad_in, w_down_t, preferred_element_type=jnp.float32)
    gate_grads = silu_grads(whole_sum(dhidden), saved_in.reshape(slot_count, 2, FF))
    expert_grad = jnp.einsum(
        "rgf,dgf->rd",
        gate_grads,
        w_gate_up.reshape(slice_width, 2, FF),
        preferred_element_type=jnp.float32,
    ).astype(jnp.bfloat16)
    returned_b = lax.all_to_all(
        expert_grad, "expert", split_axis=0, concat_axis=0, tiled=True
    ).reshape(experts, GROUP, CAP, slice_width)
    grad_sum = jnp.einsum(
        "ect,ekcd->tkd", table_bwd, returned_b, preferred_element_type=jnp.float32
    ).reshape(tok_rows, model_width)
    input_grad = (cotangent_b.astype(jnp.float32) + grad_sum).astype(jnp.bfloat16)
    grad_handoff = passed_along(input_grad, "section", -1)
    return (handoff, grad_handoff)


def solution(mesh):
    in_specs = (
        P(("section", "expert"), None),
        P(("section", "expert")),
        P(("section", "expert")),
        P(("section", "expert"), None),
        P(("section", "expert")),
        P(("section", "expert")),
        P(("section", "expert"), None),
        P(("section", "expert"), None),
        P(("section", "expert"), None),
    )
    out_specs = (P(("section", "expert"), None), P(("section", "expert"), None))
    return jax.shard_map(
        per_device, mesh=mesh, in_specs=in_specs, out_specs=out_specs, check_vma=False
    )
```

profile of v0, /device:TPU:65, one launch (start us, length us, event | category | flops | bytes accessed | tf_op | source)
XLA Modules:
  0.0 544.8 jit_solution(1958722691599542661)
XLA Ops:
  0.6 0.8 broadcast_compare_fusion.1
  1.4 0.3 reduce_window_sum.17
  1.8 2.8 fusion.30
  4.6 8.7 %all-to-all-start = ((bf16[32,12,896]{2,1,0:T(8,128)(2,1)}), bf16[32,12,896]{2,1,0:T(8,128)(2,1)S(1)}, u32[]{:S(2)}, u32[]{:S(2)}) async-start(bf16[32,12,896]{2,1,0:T(8,128)(2,1)} %bitcast.117), calls=%async_computation | async-start | bytes 1835008 | tf_op jit(solution)/shard_map/all_to_all | solution.py:63
  13.3 0.3 reduce_window_sum.18
  13.6 22.5 %all-to-all-done = bf16[32,12,896]{2,1,0:T(8,128)(2,1)S(1)} async-done(((bf16[32,12,896]{2,1,0:T(8,128)(2,1)}), bf16[32,12,896]{2,1,0:T(8,128)(2,1)S(1)}, u32[]{:S(2)}, u32[]{:S(2)}) %all-to-all-start) | async-done | bytes 688160 | tf_op jit(solution)/shard_map/all_to_all | solution.py:63
  36.3 5.6 %fusion.75 = f32[384,2048]{1,0:T(8,128)} fusion(bf16[384,896]{1,0:T(8,128)(2,1)S(1)} %all_to_all.36, bf16[896,2048]{1,0:T(8,128)(2,1)} %param.16), kind=kOutput, calls=%fused_computation.82 | convolution fusion | flops 1409286144 | bytes 7503872 | tf_op jit(solution)/shard_map/dot_general | solution.py:66
  41.9 0.6 collective-permute-start
  42.5 0.4 fusion.5
  42.9 0.3 copy.54
  43.2 0.4 fusion.41
  43.6 0.4 copy.103
  44.0 0.2 copy.38
  44.3 28.3 %all_to_all.51 = bf16[32,12,896]{2,1,0:T(8,128)(2,1)S(1)} all-to-all(bf16[32,12,896]{2,1,0:T(8,128)(2,1)S(1)} %copy.38), channel_id=1, replica_groups=mesh['section'=8,'expert'=32] {'expert'}, dimensions={0} | all-to-all | bytes 1376256 | tf_op jit(solution)/shard_map/all_to_all | solution.py:98
  72.6 1.0 all_to_all.41
  73.6 5.3 add.44
  78.9 1.0 fusion.76
  79.8 1.2 collective-permute-start.4
  81.3 1.7 broadcast_in_dim.2
  83.0 6.4 %all-to-all-start.3 = ((bf16[32,12,2048]{2,1,0:T(8,128)(2,1)}), bf16[32,12,2048]{2,1,0:T(8,128)(2,1)}, u32[]{:S(2)}, u32[]{:S(2)}) async-start(bf16[32,12,2048]{2,1,0:T(8,128)(2,1)} %bitcast.113), calls=%async_computation.3 | async-start | bytes 4194304 | tf_op jit(solution)/shard_map/all_to_all | solution.py:99
  89.4 1.7 add.49
  91.0 1.3 collective-permute-start.5
  92.3 72.8 %collective-permute-done.1 = f32[384,2048]{1,0:T(8,128)} collective-permute-done((f32[384,2048]{1,0:T(8,128)}, f32[384,2048]{1,0:T(8,128)}, u32[]{:S(2)}, u32[]{:S(2)}) %collective-permute-start.1) | collective-permute-done | bytes 3145760 | tf_op jit(solution)/shard_map/ppermute | solution.py:18
  165.1 5.2 add.45
  170.3 34.0 %collective-permute-done.5 = f32[384,1024]{1,0:T(8,128)S(1)} collective-permute-done((f32[384,1024]{1,0:T(8,128)S(1)}, f32[384,1024]{1,0:T(8,128)S(1)}, u32[]{:S(2)}, u32[]{:S(2)}) %collective-permute-start.5) | collective-permute-done | bytes 1572896 | tf_op jit(solution)/shard_map/ppermute | solution.py:18
  204.3 1.5 add.50
  205.8 4.3 reshape.139
  210.1 2.2 fusion.74
  212.3 93.2 %collective-permute-done.6 = f32[384,1024]{1,0:T(8,128)} collective-permute-done((f32[384,1024]{1,0:T(8,128)}, f32[384,1024]{1,0:T(8,128)}, u32[]{:S(2)}, u32[]{:S(2)}) %collective-permute-start.6) | collective-permute-done | bytes 1572896 | tf_op jit(solution)/shard_map/ppermute | solution.py:18
  305.5 3.3 fusion.48
  308.8 1.8 fusion.36
  310.6 1.1 all_to_all.44
  311.7 8.0 %all-to-all-start.4 = ((bf16[32,12,896]{2,1,0:T(8,128)(2,1)}), bf16[32,12,896]{2,1,0:T(8,128)(2,1)S(1)}, u32[]{:S(2)}, u32[]{:S(2)}) async-start(bf16[32,12,896]{2,1,0:T(8,128)(2,1)} %all_to_all.44), calls=%async_computation.4 | async-start | bytes 1835008 | tf_op jit(solution)/shard_map/all_to_all | solution.py:109
  319.7 5.2 add.46
  324.9 5.6 %reshape.136 = f32[384,2,1024]{2,1,0:T(2,128)} reshape(f32[384,2048]{1,0:T(8,128)} %add.46) | data formatting | bytes 6291456 | tf_op jit(solution)/shard_map/reshape | solution.py:68
  330.5 5.5 %fusion.73 = (f32[384,1,1024]{2,1,0:T(1,128)S(1)}, f32[384,1,1024]{2,1,0:T(1,128)S(1)}) fusion(f32[384,2,1024]{2,1,0:T(2,128)} %reshape.136), kind=kLoop, calls=%fused_computation.80 | loop fusion | bytes 6291456 | tf_op jit(solution)/shard_map/slice | solution.py:69
  336.1 1.3 convolution_convert_fusion.1
  337.4 1.1 all_to_all.37
  338.5 4.0 all-to-all-done.4
  342.5 6.2 %all-to-all-start.1 = ((bf16[32,12,896]{2,1,0:T(8,128)(2,1)}), bf16[32,12,896]{2,1,0:T(8,128)(2,1)}, u32[]{:S(2)}, u32[]{:S(2)}) async-start(bf16[32,12,896]{2,1,0:T(8,128)(2,1)} %all_to_all.37), calls=%async_computation.1 | async-start | bytes 1835008 | tf_op jit(solution)/shard_map/all_to_all | solution.py:73
  349.0 3.4 fusion.3
  352.4 6.4 %collective-permute-start.7 = (bf16[128,7168]{1,0:T(8,128)(2,1)}, bf16[128,7168]{1,0:T(8,128)(2,1)}, u32[]{:S(2)}, u32[]{:S(2)}) collective-permute-start(bf16[128,7168]{1,0:T(8,128)(2,1)} %fusion.3), channel_id=1, source_target_pairs={{0,224},{32,0},{64,32},{96,64},{128,96},{160,128},{192,160},{224,1... | collective-permute-start | bytes 5505032 | tf_op jit(solution)/shard_map/ppermute | solution.py:24
  358.8 91.4 %all-to-all-done.1 = bf16[32,12,896]{2,1,0:T(8,128)(2,1)} async-done(((bf16[32,12,896]{2,1,0:T(8,128)(2,1)}), bf16[32,12,896]{2,1,0:T(8,128)(2,1)}, u32[]{:S(2)}, u32[]{:S(2)}) %all-to-all-start.1) | async-done | bytes 688160 | tf_op jit(solution)/shard_map/all_to_all | solution.py:73
  450.2 1.3 copy.104
  451.7 2.3 fusion.4
  454.1 86.7 %collective-permute-done.3 = bf16[128,7168]{1,0:T(8,128)(2,1)S(1)} collective-permute-done((bf16[128,7168]{1,0:T(8,128)(2,1)S(1)}, bf16[128,7168]{1,0:T(8,128)(2,1)S(1)}, u32[]{:S(2)}, u32[]{:S(2)}) %collective-permute-start.3) | collective-permute-done | bytes 1835040 | tf_op jit(solution)/shard_map/ppermute | solution.py:24
  540.7 1.2 copy.107
  542.0 2.8 copy.108
  (33 shorter events, 1.0 us)
Async XLA Ops:
  0.6 78.2 %copy-start = (bf16[896,1024]{1,0:T(8,128)(2,1)S(1)}, bf16[896,1024]{1,0:T(8,128)(2,1)}, u32[]{:S(2)}) copy-start(bf16[896,1024]{1,0:T(8,128)(2,1)} %param.17) | copy-start | bytes 5505028
  1.8 11.5 %copy-start.5 = (s32[128]{0:T(128)S(1)}, s32[128]{0:T(128)}, u32[]{:S(2)}) copy-start(s32[128]{0:T(128)} %param.13) | copy-start | bytes 1540
  4.6 31.5 %all-to-all-start = ((bf16[32,12,896]{2,1,0:T(8,128)(2,1)}), bf16[32,12,896]{2,1,0:T(8,128)(2,1)S(1)}, u32[]{:S(2)}, u32[]{:S(2)}) async-start(bf16[32,12,896]{2,1,0:T(8,128)(2,1)} %bitcast.117), calls=%async_computation | async-start | bytes 1835008 | tf_op jit(solution)/shard_map/all_to_all | solution.py:63
  36.2 6.3 %copy-start.1 = (bf16[128,7168]{1,0:T(8,128)(2,1)S(1)}, bf16[128,7168]{1,0:T(8,128)(2,1)}, u32[]{:S(2)}) copy-start(bf16[128,7168]{1,0:T(8,128)(2,1)} %param.12) | copy-start | bytes 5505028
  36.2 6.2 %copy-start.6 = (f32[128]{0:T(128)S(1)}, f32[128]{0:T(128)}, u32[]{:S(2)}) copy-start(f32[128]{0:T(128)} %param.14) | copy-start | bytes 1540
  41.9 31.7 %collective-permute-start = (f32[384,2048]{1,0:T(8,128)}, f32[384,2048]{1,0:T(8,128)}, u32[]{:S(2)}, u32[]{:S(2)}) collective-permute-start(f32[384,2048]{1,0:T(8,128)} %fusion.75), channel_id=1, source_target_pairs={{0,1},{1,0},{2,3},{3,2},{4,5},{5,4},{6,7},{7,6},{8,9},{9,8},{10,11... | collective-permute-start | bytes 9437192 | tf_op jit(solution)/shard_map/ppermute | solution.py:18
  73.6 5.3 copy-start.2
  78.8 2.2 copy-start.3
  78.8 86.2 %collective-permute-start.1 = (f32[384,2048]{1,0:T(8,128)}, f32[384,2048]{1,0:T(8,128)}, u32[]{:S(2)}, u32[]{:S(2)}) collective-permute-start(f32[384,2048]{1,0:T(8,128)} %add.44), channel_id=1, source_target_pairs={{0,2},{2,0},{1,3},{3,1},{4,6},{6,4},{5,7},{7,5},{8,10},{10,8},{9,1... | collective-permute-start | bytes 9437192 | tf_op jit(solution)/shard_map/ppermute | solution.py:18
  79.8 9.5 %collective-permute-start.4 = (f32[384,1024]{1,0:T(8,128)S(1)}, f32[384,1024]{1,0:T(8,128)}, u32[]{:S(2)}, u32[]{:S(2)}) collective-permute-start(f32[384,1024]{1,0:T(8,128)S(1)} %fusion.76), channel_id=1, source_target_pairs={{0,1},{1,0},{2,3},{3,2},{4,5},{5,4},{6,7},{7,6},{8,9},{9,8},{10,11... | collective-permute-start | bytes 4718600 | tf_op jit(solution)/shard_map/ppermute | solution.py:18
  83.0 122.8 %all-to-all-start.3 = ((bf16[32,12,2048]{2,1,0:T(8,128)(2,1)}), bf16[32,12,2048]{2,1,0:T(8,128)(2,1)}, u32[]{:S(2)}, u32[]{:S(2)}) async-start(bf16[32,12,2048]{2,1,0:T(8,128)(2,1)} %bitcast.113), calls=%async_computation.3 | async-start | bytes 4194304 | tf_op jit(solution)/shard_map/all_to_all | solution.py:99
  91.0 113.3 %collective-permute-start.5 = (f32[384,1024]{1,0:T(8,128)S(1)}, f32[384,1024]{1,0:T(8,128)S(1)}, u32[]{:S(2)}, u32[]{:S(2)}) collective-permute-start(f32[384,1024]{1,0:T(8,128)S(1)} %add.49), channel_id=1, source_target_pairs={{0,2},{2,0},{1,3},{3,1},{4,6},{6,4},{5,7},{7,5},{8,10},{10,8},{9,1... | collective-permute-start | bytes 4718600 | tf_op jit(solution)/shard_map/ppermute | solution.py:18
  170.3 149.5 %collective-permute-start.2 = (f32[384,2048]{1,0:T(8,128)}, f32[384,2048]{1,0:T(8,128)}, u32[]{:S(2)}, u32[]{:S(2)}) collective-permute-start(f32[384,2048]{1,0:T(8,128)} %add.45), channel_id=1, source_target_pairs={{0,4},{4,0},{1,5},{5,1},{2,6},{6,2},{3,7},{7,3},{8,12},{12,8},{9,1... | collective-permute-start | bytes 9437192 | tf_op jit(solution)/shard_map/ppermute | solution.py:18
  205.8 99.7 %collective-permute-start.6 = (f32[384,1024]{1,0:T(8,128)}, f32[384,1024]{1,0:T(8,128)}, u32[]{:S(2)}, u32[]{:S(2)}) collective-permute-start(f32[384,1024]{1,0:T(8,128)} %add.50), channel_id=1, source_target_pairs={{0,4},{4,0},{1,5},{5,1},{2,6},{6,2},{3,7},{7,3},{8,12},{12,8},{9,1... | collective-permute-start | bytes 4718600 | tf_op jit(solution)/shard_map/ppermute | solution.py:18
  305.5 3.3 copy-start.7
  311.7 30.8 %all-to-all-start.4 = ((bf16[32,12,896]{2,1,0:T(8,128)(2,1)}), bf16[32,12,896]{2,1,0:T(8,128)(2,1)S(1)}, u32[]{:S(2)}, u32[]{:S(2)}) async-start(bf16[32,12,896]{2,1,0:T(8,128)(2,1)} %all_to_all.44), calls=%async_computation.4 | async-start | bytes 1835008 | tf_op jit(solution)/shard_map/all_to_all | solution.py:109
  342.5 107.7 %all-to-all-start.1 = ((bf16[32,12,896]{2,1,0:T(8,128)(2,1)}), bf16[32,12,896]{2,1,0:T(8,128)(2,1)}, u32[]{:S(2)}, u32[]{:S(2)}) async-start(bf16[32,12,896]{2,1,0:T(8,128)(2,1)} %all_to_all.37), calls=%async_computation.1 | async-start | bytes 1835008 | tf_op jit(solution)/shard_map/all_to_all | solution.py:73
  352.4 99.3 %copy-start.4 = (f32[128]{0:T(128)S(1)}, f32[128]{0:T(128)}, u32[]{:S(2)}) copy-start(f32[128]{0:T(128)} %param.11) | copy-start | bytes 1540
  352.4 101.6 %collective-permute-start.7 = (bf16[128,7168]{1,0:T(8,128)(2,1)}, bf16[128,7168]{1,0:T(8,128)(2,1)}, u32[]{:S(2)}, u32[]{:S(2)}) collective-permute-start(bf16[128,7168]{1,0:T(8,128)(2,1)} %fusion.3), channel_id=1, source_target_pairs={{0,224},{32,0},{64,32},{96,64},{128,96},{160,128},{192,160},{224,1... | collective-permute-start | bytes 5505032 | tf_op jit(solution)/shard_map/ppermute | solution.py:24
  454.0 86.8 %collective-permute-start.3 = (bf16[128,7168]{1,0:T(8,128)(2,1)S(1)}, bf16[128,7168]{1,0:T(8,128)(2,1)S(1)}, u32[]{:S(2)}, u32[]{:S(2)}) collective-permute-start(bf16[128,7168]{1,0:T(8,128)(2,1)S(1)} %fusion.4), channel_id=1, source_target_pairs={{0,32},{32,64},{64,96},{96,128},{128,160},{160,192},{192,224},{224... | collective-permute-start | bytes 5505032 | tf_op jit(solution)/shard_map/ppermute | solution.py:24
where the time goes:
time: 548 us; the launch traced here: 545 us
  waiting for transfers between devices  404 us (74%)
  starting transfers between devices  38.9 us (7%)
  local copies, waits for them, and re-layouts  29.4 us (5%)
  blocking collectives  28.3 us (5%)
  other arithmetic  23.9 us (4%)
  matrix products  18.9 us (3%)
    ppermute x6, waiting for transfers between devices, swapped(): return lax.ppermute(block, axis, route)  200 us
    all_to_all x1, waiting for transfers between devices, per_device(): lax.all_to_all(expert_out, 'expert', split_axis=0, concat_axis=0, tiled=T...  91.4 us
    ppermute x2, waiting for transfers between devices, passed_along(): return lax.ppermute(value, axis, pairs)  86.7 us
    all_to_all x1, blocking collectives, per_device(): lax.all_to_all(grad_out, 'expert', split_axis=0, concat_axis=0, tiled=True)  28.3 us
    all_to_all x1, waiting for transfers between devices, per_device(): lax.all_to_all(outbound.reshape(-1, slice_width), 'expert', split_axis=0,...  22.5 us
    add x5, other arithmetic, whole_sum(): partial_value = partial_value + swapped(partial_value, 'expert', bit_index)  18.8 us
  transfers between devices with their start and end apart: 12, of which 7 were waited for; matrix products, arithmetic and copies ran while one was open for 9% of the time, Pallas kernels for 0%

commit v1 on v0

v1 whole, which is shorter than its diff:
```python
import functools

import jax
import jax.numpy as jnp
import numpy as np
from jax import lax
from jax.experimental import pallas as pl
from jax.experimental.pallas import tpu as pltpu
from jax.sharding import PartitionSpec as P

FF = 1024
GROUP = 8
CAP = 12
EXPERTS = 4
SLOTS = EXPERTS * CAP
TOK = 128
EARLY = TOK - SLOTS
D = 7168
SL = D // GROUP
HC = FF // GROUP
ROWS = GROUP * SLOTS
ZROWS = GROUP * CAP
BF = jnp.bfloat16
F32 = jnp.float32
SUM_T = jnp.bfloat16
PAIRS = [(2, 0), (2, 1), (1, 0), (1, 1), (3, 0), (3, 1), (0, 1)]


def regroup_matrix():
    row = np.arange(ROWS)
    expert, peer, slot = row // ZROWS, (row % ZROWS) // CAP, row % CAP
    column = peer * SLOTS + expert * CAP + slot
    table = np.zeros((ROWS, ROWS), np.float32)
    table[row, column] = 1.0
    return table


def nt_dot(left, right):
    return lax.dot_general(left, right, (((1,), (1,)), ((), ())), preferred_element_type=F32)


def nn_dot(left, right):
    return jnp.dot(left, right, preferred_element_type=F32)


def iota(shape, dim):
    return lax.broadcasted_iota(jnp.int32, shape, dim)


def slot_positions(routes):
    match = (routes == iota((8, TOK), 0)).astype(F32)
    upper = (iota((TOK, TOK), 0) <= iota((TOK, TOK), 1)).astype(BF)
    rank = nn_dot(match.astype(BF), upper) - 1.0
    counts = jnp.sum(match, axis=1, keepdims=True)
    spare = rank[EXPERTS : EXPERTS + 1] - EARLY
    placed = jnp.zeros((1, TOK), F32)
    leftover = jnp.zeros((1, TOK), F32)
    before = jnp.zeros((1, 1), F32)
    for expert in range(EXPERTS):
        own = match[expert : expert + 1]
        count = counts[expert : expert + 1]
        placed = placed + own * (CAP * expert + rank[expert : expert + 1])
        after = before + (CAP - count)
        inside = (spare >= before) & (spare < after)
        leftover = leftover + jnp.where(inside, CAP * expert + count + (spare - before), 0.0)
        before = after
    outside = jnp.where(spare < 0.0, spare + TOK, leftover)
    return placed + match[EXPERTS : EXPERTS + 1] * outside


def slot_matrix(routes, scale):
    pos = slot_positions(routes)
    hit = iota((TOK, TOK), 0).astype(F32) == pos
    kept = jnp.where(routes < EXPERTS, scale, 0.0)
    column = jnp.sum(jnp.where(hit, kept, 0.0), axis=1, keepdims=True)
    eye = iota((TOK, TOK), 0) == iota((TOK, TOK), 1)
    row = jnp.sum(jnp.where(eye, column, 0.0), axis=0, keepdims=True)
    return hit.astype(BF), row


def kernel(
    routes_a, scale_a, routes_b, scale_b, x_hbm, cot_hbm, saved_hbm, wgu_hbm, wd_hbm, regroup_hbm,
    rows_a, rows_b, perm_a, perm_b,
    x_v, cot_v, saved_v, wgu, wd, regroup,
    pm_a, pm_b, sc_out, sc_in,
    pk_a, pk_b, early_a, early_b,
    r1_a, r1_b, s2_a, s2_b, r2_a, r2_b,
    ps_a, ps_b, own_a, own_b, rs_a, rs_b,
    h_a, g_b, eo_a, eo_b, r3_a, r3_b, s4_a, s4_b,
    load_sem,
    sc_ss, sc_rs, d1a_ss, d1a_rs, d1b_ss, d1b_rs, d2a_ss, d2a_rs, d2b_ss, d2b_rs,
    rsa_ss, rsa_rs, rsb_ss, rsb_rs, aga_ss, aga_rs, agb_ss, agb_rs,
    rta_ss, rta_rs, rtb_ss, rtb_rs, fa_ss, fa_rs, fb_ss, fb_rs, e_ss, e_rs,
):
    section = lax.axis_index("section")
    place = lax.axis_index("expert")
    layer = place // GROUP
    me = place % GROUP
    y = me // 2
    core = me % 2
    n_sec = lax.axis_size("section")
    ahead = (section + 1) % n_sec
    behind = (section + n_sec - 1) % n_sec

    def peer(pair):
        return ((y + pair[0]) % 4) * 2 + (core + pair[1]) % 2

    def plane_dev(pair):
        return (section, layer * GROUP + peer(pair))

    def depth(step):
        return (layer + step) % EXPERTS

    def depth_dev(step):
        return (section, depth(step) * GROUP + me)

    def remote(src, dst, ss, rs, dev):
        return pltpu.make_async_remote_copy(
            src_ref=src, dst_ref=dst, send_sem=ss, recv_sem=rs,
            device_id=dev, device_id_type=pl.DeviceIdType.MESH,
        )

    barrier = pltpu.get_barrier_semaphore()
    greeted = [plane_dev(pair) for pair in PAIRS] + [depth_dev(step) for step in (1, 2, 3)]
    for other in range(GROUP):
        greeted.append((ahead, layer * GROUP + other))
        greeted.append((behind, layer * GROUP + other))
    for dev in greeted:
        pl.semaphore_signal(barrier, 1, device_id=dev, device_id_type=pl.DeviceIdType.MESH)

    loads = []
    for i, (src, dst) in enumerate(
        [(x_hbm, x_v), (cot_hbm, cot_v), (saved_hbm, saved_v), (regroup_hbm, regroup),
         (wgu_hbm, wgu), (wd_hbm, wd)]
    ):
        copy = pltpu.make_async_copy(src, dst, load_sem.at[i])
        copy.start()
        loads.append(copy)

    mat_a, row_a = slot_matrix(routes_a[...], scale_a[...])
    mat_b, row_b = slot_matrix(routes_b[...], scale_b[...])
    pm_a[...] = mat_a
    pm_b[...] = mat_b
    line = iota((8, TOK), 0)
    sc_out[...] = jnp.where(line == 0, row_a, jnp.where(line == 1, row_b, 0.0))
    sc_in[me] = sc_out[...]

    pending = []

    loads[0].wait()
    for part in range(GROUP):
        cols = slice(part * SL, (part + 1) * SL)
        packed = nn_dot(pm_a[...], x_v[:, cols]).astype(BF)
        pk_a[part] = packed[:SLOTS]
        early_a[:, cols] = packed[SLOTS:]
    pl.semaphore_wait(barrier, len(greeted))

    def plane_sends(items):
        out = []
        for i, pair in enumerate(PAIRS):
            for src, dst, ss, rs in items(pair):
                copy = remote(src, dst, ss.at[i], rs.at[i], plane_dev(pair))
                copy.start()
                out.append(copy)
                pending.append(copy)
        return out

    in_1a = plane_sends(lambda pair: [
        (pk_a.at[peer(pair)], r1_a.at[me], d1a_ss, d1a_rs),
        (sc_out, sc_in.at[me], sc_ss, sc_rs),
    ])
    r1_a[me] = pk_a[me]

    loads[1].wait()
    loads[2].wait()
    for part in range(GROUP):
        cols = slice(part * SL, (part + 1) * SL)
        packed = nn_dot(pm_b[...], cot_v[:, cols]).astype(BF)
        pk_b[part, :, :SL] = packed[:SLOTS]
        early_b[:, cols] = packed[SLOTS:]
        for half in range(2):
            first = half * FF + part * HC
            picked = nn_dot(pm_b[:SLOTS, :], saved_v[:, first : first + HC]).astype(BF)
            pk_b[part, :, SL + half * HC : SL + (half + 1) * HC] = picked
    in_1b = plane_sends(lambda pair: [(pk_b.at[peer(pair)], r1_b.at[me], d1b_ss, d1b_rs)])
    r1_b[me] = pk_b[me]

    def scale_column(which):
        mask = iota((SLOTS, TOK), 0) == iota((SLOTS, TOK), 1)
        return [
            jnp.sum(jnp.where(mask, sc_in[p, which : which + 1, :], 0.0), axis=1, keepdims=True)
            for p in range(GROUP)
        ]

    def depth_sends(src, dst, ss, rs):
        out = []
        for i, step in enumerate((2, 1, 3)):
            copy = remote(src.at[depth(step)], dst.at[layer], ss.at[i], rs.at[i], depth_dev(step))
            copy.start()
            out.append(copy)
            pending.append(copy)
        return out

    for copy in in_1a:
        copy.wait_recv()
    loads[3].wait()
    moved = nn_dot(regroup[...], r1_a[...].reshape(ROWS, SL)).astype(BF)
    s2_a[...] = moved.reshape(EXPERTS, ZROWS, SL)
    in_2a = depth_sends(s2_a, r2_a, d2a_ss, d2a_rs)
    r2_a[layer] = s2_a[layer]

    for copy in in_1b:
        copy.wait_recv()
    columns = scale_column(1)
    scaled = jnp.concatenate(
        [(columns[p] * r1_b[p, :, :SL].astype(F32)).astype(BF) for p in range(GROUP)], axis=0
    )
    s2_b[:, :, :SL] = nn_dot(regroup[...], scaled).astype(BF).reshape(EXPERTS, ZROWS, SL)
    carried = r1_b[:, :, SL:].reshape(ROWS, 2 * HC)
    s2_b[:, :, SL:] = nn_dot(regroup[...], carried).astype(BF).reshape(EXPERTS, ZROWS, 2 * HC)
    in_2b = depth_sends(s2_b, r2_b, d2b_ss, d2b_rs)
    r2_b[layer] = s2_b[layer]

    finals = []
    for i, (src, dst, sec) in enumerate([
        (early_a, rows_a.at[pl.ds(SLOTS, EARLY), :], ahead),
        (early_b, rows_b.at[pl.ds(SLOTS, EARLY), :], behind),
        (pm_a, perm_a, ahead),
        (pm_b, perm_b, behind),
    ]):
        copy = remote(src, dst, e_ss.at[i], e_rs.at[i], (sec, place))
        copy.start()
        finals.append(copy)
        pending.append(copy)

    for copy in in_2a:
        copy.wait_recv()
    loads[4].wait()
    loads[5].wait()
    in_rsa = []
    for i, d in enumerate((2, 1, 3, 0)):
        chip = (y + d) % 4
        acts = r2_a[...].reshape(ROWS, SL)
        first = pl.multiple_of(chip * (2 * HC), 2 * HC)
        gate = nn_dot(acts, wgu[:, pl.ds(first, 2 * HC)])
        second = pl.multiple_of(FF + chip * (2 * HC), 2 * HC)
        up = nn_dot(acts, wgu[:, pl.ds(second, 2 * HC)])
        for c in range(2):
            cols = slice(c * HC, (c + 1) * HC)
            ps_a[d, c, :, :HC] = gate[:, cols].astype(SUM_T)
            ps_a[d, c, :, HC:] = up[:, cols].astype(SUM_T)
            if d == 0:
                own_a[c, :, :HC] = gate[:, cols]
                own_a[c, :, HC:] = up[:, cols]
        for cc in range(2):
            if (d, cc) != (0, 0):
                k = PAIRS.index((d, cc))
                copy = remote(ps_a.at[d, (core + cc) % 2], rs_a.at[k], rsa_ss.at[k], rsa_rs.at[k], plane_dev((d, cc)))
                copy.start()
                in_rsa.append(copy)
                pending.append(copy)

    for copy in in_2b:
        copy.wait_recv()
    in_rsb = []
    for i, d in enumerate((2, 1, 3, 0)):
        chip = (y + d) % 4
        acts = r2_b[:, :, :SL].reshape(ROWS, SL)
        first = pl.multiple_of(chip * (2 * HC), 2 * HC)
        part = nn_dot(acts, wd[:, pl.ds(first, 2 * HC)])
        for c in range(2):
            cols = slice(c * HC, (c + 1) * HC)
            ps_b[d, c] = part[:, cols].astype(SUM_T)
            if d == 0:
                own_b[c] = part[:, cols]
        for cc in range(2):
            if (d, cc) != (0, 0):
                k = PAIRS.index((d, cc))
                copy = remote(ps_b.at[d, (core + cc) % 2], rs_b.at[k], rsb_ss.at[k], rsb_rs.at[k], plane_dev((d, cc)))
                copy.start()
                in_rsb.append(copy)
                pending.append(copy)

    for copy in in_rsa:
        copy.wait_recv()
    total = own_a[core]
    for k in range(len(PAIRS)):
        total = total + rs_a[k].astype(F32)
    gate, up = total[:, :HC], total[:, HC:]
    h_a[me] = (gate * jax.nn.sigmoid(gate) * up).astype(BF)
    in_aga = plane_sends(lambda pair: [(h_a.at[me], h_a.at[me], aga_ss, aga_rs)])

    for copy in in_rsb:
        copy.wait_recv()
    dhid = own_b[core]
    for k in range(len(PAIRS)):
        dhid = dhid + rs_b[k].astype(F32)
    held = r2_b[:, :, SL:].reshape(ROWS, 2 * HC).astype(F32)
    gate, up = held[:, :HC], held[:, HC:]
    sig = jax.nn.sigmoid(gate)
    g_b[me, :, :HC] = (dhid * up * sig * (1.0 + gate * (1.0 - sig))).astype(BF)
    g_b[me, :, HC:] = (dhid * gate * sig).astype(BF)
    in_agb = plane_sends(lambda pair: [(g_b.at[me], g_b.at[me], agb_ss, agb_rs)])

    for copy in in_aga:
        copy.wait_recv()
    hidden = jnp.concatenate([h_a[p] for p in range(GROUP)], axis=1)
    for q in range(0, SL, 128):
        out = nt_dot(hidden, wd[q : q + 128, :]).astype(BF)
        eo_a[:, :, q : q + 128] = out.reshape(EXPERTS, ZROWS, 128)
    in_3a = depth_sends(eo_a, r3_a, rta_ss, rta_rs)
    r3_a[layer] = eo_a[layer]

    for copy in in_agb:
        copy.wait_recv()
    left = jnp.concatenate([g_b[p, :, :HC] for p in range(GROUP)], axis=1)
    right = jnp.concatenate([g_b[p, :, HC:] for p in range(GROUP)], axis=1)
    for q in range(0, SL, 128):
        out = nt_dot(left, wgu[q : q + 128, :FF]) + nt_dot(right, wgu[q : q + 128, FF:])
        eo_b[:, :, q : q + 128] = out.astype(BF).reshape(EXPERTS, ZROWS, 128)
    in_3b = depth_sends(eo_b, r3_b, rtb_ss, rtb_rs)
    r3_b[layer] = eo_b[layer]

    def last_sends(src, dst, ss, rs, sec):
        lane = pl.multiple_of(me * SL, SL)
        for p in range(GROUP):
            other = (me + p) % GROUP
            copy = remote(
                src.at[other], dst.at[pl.ds(0, SLOTS), pl.ds(lane, SL)],
                ss.at[p], rs.at[p], (sec, layer * GROUP + other),
            )
            copy.start()
            finals.append(copy)
            pending.append(copy)

    def back(ref):
        return lax.dot_general(
            regroup[...], ref[...].reshape(ROWS, SL), (((0,), (0,)), ((), ())),
            preferred_element_type=F32,
        ).reshape(GROUP, SLOTS, SL)

    for copy in in_3a:
        copy.wait_recv()
    columns = scale_column(0)
    came = back(r3_a)
    for p in range(GROUP):
        s4_a[p] = (r1_a[p].astype(F32) + columns[p] * came[p]).astype(BF)
    last_sends(s4_a, rows_a, fa_ss, fa_rs, ahead)

    for copy in in_3b:
        copy.wait_recv()
    came = back(r3_b)
    for p in range(GROUP):
        s4_b[p] = (r1_b[p, :, :SL].astype(F32) + came[p]).astype(BF)
    last_sends(s4_b, rows_b, fb_ss, fb_rs, behind)

    for copy in finals:
        copy.wait_recv()
    for copy in pending:
        copy.wait_send()


def relay_layer(routes_a, scale_a, routes_b, scale_b, x, cot, saved, wgu, wd):
    vmem, hbm = pl.BlockSpec(memory_space=pltpu.VMEM), pl.BlockSpec(memory_space=pl.ANY)
    dma = pltpu.SemaphoreType.DMA
    v = pltpu.VMEM
    n = len(PAIRS)
    wide = SL + 2 * HC
    scratch = [
        v((TOK, D), BF), v((TOK, D), BF), v((TOK, 2 * FF), BF), v((SL, 2 * FF), BF), v((SL, FF), BF), v((ROWS, ROWS), BF),
        v((TOK, TOK), BF), v((TOK, TOK), BF), v((8, TOK), F32), v((GROUP, 8, TOK), F32),
        v((GROUP, SLOTS, SL), BF), v((GROUP, SLOTS, wide), BF), v((EARLY, D), BF), v((EARLY, D), BF),
        v((GROUP, SLOTS, SL), BF), v((GROUP, SLOTS, wide), BF),
        v((EXPERTS, ZROWS, SL), BF), v((EXPERTS, ZROWS, wide), BF),
        v((EXPERTS, ZROWS, SL), BF), v((EXPERTS, ZROWS, wide), BF),
        v((4, 2, ROWS, 2 * HC), SUM_T), v((4, 2, ROWS, HC), SUM_T), v((2, ROWS, 2 * HC), F32), v((2, ROWS, HC), F32),
        v((n, ROWS, 2 * HC), SUM_T), v((n, ROWS, HC), SUM_T),
        v((GROUP, ROWS, HC), BF), v((GROUP, ROWS, 2 * HC), BF),
        v((EXPERTS, ZROWS, SL), BF), v((EXPERTS, ZROWS, SL), BF),
        v((EXPERTS, ZROWS, SL), BF), v((EXPERTS, ZROWS, SL), BF),
        v((GROUP, SLOTS, SL), BF), v((GROUP, SLOTS, SL), BF),
        dma((6,)),
    ]
    for size in (n, n, n, 3, 3, n, n, n, n, 3, 3, GROUP, GROUP, 4):
        scratch += [dma((size,)), dma((size,))]
    return pl.pallas_call(
        kernel,
        out_shape=[
            jax.ShapeDtypeStruct((TOK, D), BF), jax.ShapeDtypeStruct((TOK, D), BF),
            jax.ShapeDtypeStruct((TOK, TOK), BF), jax.ShapeDtypeStruct((TOK, TOK), BF),
        ],
        in_specs=[vmem] * 4 + [hbm] * 6,
        out_specs=[hbm] * 4,
        scratch_shapes=scratch,
        compiler_params=pltpu.CompilerParams(
            collective_id=0, has_side_effects=True, vmem_limit_bytes=56 << 20
        ),
        name="expert_relay",
    )(routes_a, scale_a, routes_b, scale_b, x, cot, saved, wgu, wd, jnp.asarray(regroup_matrix(), BF))


def per_device(x_a, routes_a, scale_a, cotangent_b, routes_b, scale_b, saved_b, w_gate_up, w_down_t):
    rows_a, rows_b, perm_a, perm_b = relay_layer(
        routes_a.reshape(1, TOK), scale_a.reshape(1, TOK), routes_b.reshape(1, TOK), scale_b.reshape(1, TOK),
        x_a, cotangent_b, saved_b, w_gate_up, w_down_t,
    )
    put = lambda perm, rows: jnp.einsum("rt,rd->td", perm, rows, preferred_element_type=F32).astype(BF)
    return put(perm_a, rows_a), put(perm_b, rows_b)


def solution(mesh):
    both = ("section", "expert")
    mat, vec = P(both, None), P(both)
    return jax.shard_map(
        per_device, mesh=mesh, in_specs=(mat, vec, vec, mat, vec, vec, mat, mat, mat),
        out_specs=(mat, mat), check_vma=False,
    )
```

time: 548 us -> 217 us (0.40)
  the two profiles are of different devices: /device:TPU:65 before, /device:TPU:197 now
where the time goes in v1:
time: 217 us; the launch traced here: 216 us
  Pallas kernels  210 us (97%)
  matrix products  5.44 us (3%)
    pallas_call x1, Pallas kernels, relay_layer(): pl.pallas_call(kernel, out_shape=[jax.ShapeDtypeStruct((TOK, D), BF), jax...  210 us
    dot_general x2, matrix products, per_device(): jnp.einsum('rt,rd->td', perm, rows, preferred_element_type=F32).astype(BF)  5.44 us

profile of v1, /device:TPU:197, one launch (start us, length us, event | category | flops | bytes accessed | tf_op | source)
XLA Modules:
  0.0 216.4 jit_solution(10300126999355634119)
XLA Ops:
  0.6 210.3 %expert_relay.1 = (bf16[128,7168]{1,0:T(8,128)(2,1)}, bf16[128,7168]{1,0:T(8,128)(2,1)}, bf16[128,128]{1,0:T(8,128)(2,1)}, bf16[128,128]{1,0:T(8,128)(2,1)}) custom-call(s32[1,128]{1,0:T(1,128)} %bitcast.8, f32[1,128]{1,0:T(1,128)} %bitcast.9, s32[1,128]{1,0:T(1,128)} %bitcast.10, f32[1,128]{1,0:T(1,128)} %bitcast.11, bf16[128,7168]{1,0:T(8,128)(2,1)} %x_hbm.1, ...), custom_call_target="tpu_custom_call" | custom-call | tf_op jit(solution)/shard_map/expert_relay/pallas_call | solution.py:386
  211.0 0.0 copy-start
  211.0 0.0 copy-start.1
  211.0 3.5 %convolution_convert_fusion.1 = bf16[128,7168]{1,0:T(8,128)(2,1)} fusion(bf16[128,128]{1,0:T(8,128)(2,1)} %get-tuple-element.6, bf16[128,7168]{1,0:T(8,128)(2,1)} %get-tuple-element.7), kind=kOutput, calls=%fused_computation.1 | convolution fusion | flops 235798528 | bytes 3702784 | tf_op jit(solution)/shard_map/rt,rd->td/dot_general | solution.py:407
  214.5 0.0 copy-done
  214.5 0.0 copy-done.1
  214.6 1.9 convolution_convert_fusion
Async XLA Ops:
  211.0 3.6 %copy-start = (bf16[128,7168]{1,0:T(8,128)(2,1)S(1)}, bf16[128,7168]{1,0:T(8,128)(2,1)}, u32[]{:S(2)}) copy-start(bf16[128,7168]{1,0:T(8,128)(2,1)} %get-tuple-element.9) | copy-start | bytes 5505028
  211.0 3.6 %copy-start.1 = (bf16[128,128]{1,0:T(8,128)(2,1)S(1)}, bf16[128,128]{1,0:T(8,128)(2,1)}, u32[]{:S(2)}) copy-start(bf16[128,128]{1,0:T(8,128)(2,1)} %get-tuple-element.8) | copy-start | bytes 98308

commit v2 on v1

--- a/solution.py
+++ b/solution.py
@@ -23,6 +23,7 @@
 BF = jnp.bfloat16
 F32 = jnp.float32
 SUM_T = jnp.bfloat16
+PIECES = [(0, 16), (16, 32), (48, 32)]
 PAIRS = [(2, 0), (2, 1), (1, 0), (1, 1), (3, 0), (3, 1), (0, 1)]
 
 
@@ -85,12 +86,12 @@
     pm_a, pm_b, sc_out, sc_in,
     pk_a, pk_b, early_a, early_b,
     r1_a, r1_b, s2_a, s2_b, r2_a, r2_b,
-    ps_a, ps_b, own_a, own_b, rs_a, rs_b,
-    h_a, g_b, eo_a, eo_b, r3_a, r3_b, s4_a, s4_b,
+    ps_a, ps_b, sib_a, sib_b, sum_a, sum_b, rs_a, rs_b,
+    h_a, g_b, eo_a, eo_b, r3_a, r3_b, s4_a, s4_b, rl_a, rl_b,
     load_sem,
     sc_ss, sc_rs, d1a_ss, d1a_rs, d1b_ss, d1b_rs, d2a_ss, d2a_rs, d2b_ss, d2b_rs,
-    rsa_ss, rsa_rs, rsb_ss, rsb_rs, aga_ss, aga_rs, agb_ss, agb_rs,
-    rta_ss, rta_rs, rtb_ss, rtb_rs, fa_ss, fa_rs, fb_ss, fb_rs, e_ss, e_rs,
+    sba_ss, sba_rs, sbb_ss, sbb_rs, rsa_ss, rsa_rs, rsb_ss, rsb_rs, aga_ss, aga_rs, agb_ss, agb_rs,
+    rta_ss, rta_rs, rtb_ss, rtb_rs, fa_ss, fa_rs, fb_ss, fb_rs, e_ss, e_rs, rl_ss, rl_rs,
 ):
     section = lax.axis_index("section")
     place = lax.axis_index("expert")
@@ -102,6 +103,12 @@
     ahead = (section + 1) % n_sec
     behind = (section + n_sec - 1) % n_sec
 
+    x = section % 4
+    edges = {0: x == 3, 1: x == 0}
+
+    def sec_at(step):
+        return (section + step + n_sec) % n_sec
+
     def peer(pair):
         return ((y + pair[0]) % 4) * 2 + (core + pair[1]) % 2
 
@@ -122,9 +129,10 @@
 
     barrier = pltpu.get_barrier_semaphore()
     greeted = [plane_dev(pair) for pair in PAIRS] + [depth_dev(step) for step in (1, 2, 3)]
-    for other in range(GROUP):
-        greeted.append((ahead, layer * GROUP + other))
-        greeted.append((behind, layer * GROUP + other))
+    greeted += [(sec_at(step), place) for step in range(1, 8)]
+    for other in range(1, GROUP):
+        greeted.append((ahead, layer * GROUP + (me + other) % GROUP))
+        greeted.append((behind, layer * GROUP + (me + other) % GROUP))
     for dev in greeted:
         pl.semaphore_signal(barrier, 1, device_id=dev, device_id_type=pl.DeviceIdType.MESH)
 
@@ -134,7 +142,8 @@
          (wgu_hbm, wgu), (wd_hbm, wd)]
     ):
         copy = pltpu.make_async_copy(src, dst, load_sem.at[i])
-        copy.start()
+        if i < 4:
+            copy.start()
         loads.append(copy)
 
     mat_a, row_a = slot_matrix(routes_a[...], scale_a[...])
@@ -146,13 +155,68 @@
     sc_in[me] = sc_out[...]
 
     pending = []
+    finals = []
+    guarded = []
+
+    def when_send(cond, copy):
+        pl.when(cond)(copy.start)
+        guarded.append((cond, copy))
+
+    rows_of = {0: rows_a, 1: rows_b}
+    early_of = {0: early_a, 1: early_b}
+    relay_of = {0: rl_a, 1: rl_b}
+    sign = {0: 1, 1: -1}
+
+    def early_copy(b, i, src, step):
+        first, size = PIECES[i]
+        return remote(src, rows_of[b].at[pl.ds(SLOTS + first, size), :],
+                      e_ss.at[b, i], e_rs.at[b, i], (sec_at(step), place))
+
+    def own_piece(b, i):
+        first, size = PIECES[i]
+        return early_of[b].at[pl.ds(first, size), :]
+
+    def early_start(b):
+        copy = early_copy(b, 0, own_piece(b, 0), sign[b])
+        copy.start()
+        pending.append(copy)
+        for i in (1, 2):
+            copy = remote(own_piece(b, i), relay_of[b], e_ss.at[b, i], rl_rs.at[b],
+                          (sec_at(-i * sign[b]), place))
+            when_send(edges[b], copy)
+
+    def early_direct():
+        for b in (0, 1):
+            for i in (1, 2):
+                when_send(jnp.logical_not(edges[b]), early_copy(b, i, own_piece(b, i), sign[b]))
+        for b, (src, dst) in enumerate(((pm_a, perm_a), (pm_b, perm_b))):
+            copy = remote(src, dst, e_ss.at[b, 3], e_rs.at[b, 3], (sec_at(sign[b]), place))
+            copy.start()
+            finals.append(copy)
+            pending.append(copy)
+
+    def early_relay(b):
+        for i in (1, 2):
+            there = x == (3 - i if b == 0 else i)
+            copy = remote(relay_of[b], rows_of[b].at[pl.ds(SLOTS + PIECES[i][0], PIECES[i][1]), :],
+                          rl_ss.at[b], e_rs.at[b, i], (sec_at((i + 1) * sign[b]), place))
+
+            @pl.when(there)
+            def _():
+                remote(relay_of[b], relay_of[b], rl_ss.at[b], rl_rs.at[b], (sec_at(1), place)).wait_recv()
+                copy.start()
+
+            guarded.append((there, copy))
 
     loads[0].wait()
-    for part in range(GROUP):
-        cols = slice(part * SL, (part + 1) * SL)
+
+    @pl.loop(0, GROUP)
+    def _(part):
+        cols = pl.ds(pl.multiple_of(part * SL, SL), SL)
         packed = nn_dot(pm_a[...], x_v[:, cols]).astype(BF)
         pk_a[part] = packed[:SLOTS]
         early_a[:, cols] = packed[SLOTS:]
+
     pl.semaphore_wait(barrier, len(greeted))
 
     def plane_sends(items):
@@ -169,20 +233,27 @@
         (pk_a.at[peer(pair)], r1_a.at[me], d1a_ss, d1a_rs),
         (sc_out, sc_in.at[me], sc_ss, sc_rs),
     ])
+    early_start(0)
     r1_a[me] = pk_a[me]
+    loads[4].start()
+    loads[5].start()
 
     loads[1].wait()
     loads[2].wait()
-    for part in range(GROUP):
-        cols = slice(part * SL, (part + 1) * SL)
+
+    @pl.loop(0, GROUP)
+    def _(part):
+        cols = pl.ds(pl.multiple_of(part * SL, SL), SL)
         packed = nn_dot(pm_b[...], cot_v[:, cols]).astype(BF)
         pk_b[part, :, :SL] = packed[:SLOTS]
         early_b[:, cols] = packed[SLOTS:]
-        for half in range(2):
-            first = half * FF + part * HC
-            picked = nn_dot(pm_b[:SLOTS, :], saved_v[:, first : first + HC]).astype(BF)
-            pk_b[part, :, SL + half * HC : SL + (half + 1) * HC] = picked
+        first = pl.multiple_of(part * HC, HC)
+        second = pl.multiple_of(FF + part * HC, HC)
+        held = jnp.concatenate([saved_v[:, pl.ds(first, HC)], saved_v[:, pl.ds(second, HC)]], axis=1)
+        pk_b[part, :, SL:] = nn_dot(pm_b[:SLOTS, :], held).astype(BF)
+
     in_1b = plane_sends(lambda pair: [(pk_b.at[peer(pair)], r1_b.at[me], d1b_ss, d1b_rs)])
+    early_start(1)
     r1_b[me] = pk_b[me]
 
     def scale_column(which):
@@ -221,86 +292,80 @@
     in_2b = depth_sends(s2_b, r2_b, d2b_ss, d2b_rs)
     r2_b[layer] = s2_b[layer]
 
-    finals = []
-    for i, (src, dst, sec) in enumerate([
-        (early_a, rows_a.at[pl.ds(SLOTS, EARLY), :], ahead),
-        (early_b, rows_b.at[pl.ds(SLOTS, EARLY), :], behind),
-        (pm_a, perm_a, ahead),
-        (pm_b, perm_b, behind),
-    ]):
-        copy = remote(src, dst, e_ss.at[i], e_rs.at[i], (sec, place))
-        copy.start()
-        finals.append(copy)
-        pending.append(copy)
+    early_direct()
 
     for copy in in_2a:
         copy.wait_recv()
     loads[4].wait()
     loads[5].wait()
-    in_rsa = []
-    for i, d in enumerate((2, 1, 3, 0)):
-        chip = (y + d) % 4
-        acts = r2_a[...].reshape(ROWS, SL)
-        first = pl.multiple_of(chip * (2 * HC), 2 * HC)
-        gate = nn_dot(acts, wgu[:, pl.ds(first, 2 * HC)])
-        second = pl.multiple_of(FF + chip * (2 * HC), 2 * HC)
-        up = nn_dot(acts, wgu[:, pl.ds(second, 2 * HC)])
-        for c in range(2):
-            cols = slice(c * HC, (c + 1) * HC)
-            ps_a[d, c, :, :HC] = gate[:, cols].astype(SUM_T)
-            ps_a[d, c, :, HC:] = up[:, cols].astype(SUM_T)
-            if d == 0:
-                own_a[c, :, :HC] = gate[:, cols]
-                own_a[c, :, HC:] = up[:, cols]
-        for cc in range(2):
-            if (d, cc) != (0, 0):
-                k = PAIRS.index((d, cc))
-                copy = remote(ps_a.at[d, (core + cc) % 2], rs_a.at[k], rsa_ss.at[k], rsa_rs.at[k], plane_dev((d, cc)))
-                copy.start()
-                in_rsa.append(copy)
-                pending.append(copy)
-
-    for copy in in_2b:
-        copy.wait_recv()
-    in_rsb = []
-    for i, d in enumerate((2, 1, 3, 0)):
-        chip = (y + d) % 4
-        acts = r2_b[:, :, :SL].reshape(ROWS, SL)
-        first = pl.multiple_of(chip * (2 * HC), 2 * HC)
-        part = nn_dot(acts, wd[:, pl.ds(first, 2 * HC)])
-        for c in range(2):
-            cols = slice(c * HC, (c + 1) * HC)
-            ps_b[d, c] = part[:, cols].astype(SUM_T)
-            if d == 0:
-                own_b[c] = part[:, cols]
-        for cc in range(2):
-            if (d, cc) != (0, 0):
-                k = PAIRS.index((d, cc))
-                copy = remote(ps_b.at[d, (core + cc) % 2], rs_b.at[k], rsb_ss.at[k], rsb_rs.at[k], plane_dev((d, cc)))
-                copy.start()
-                in_rsb.append(copy)
-                pending.append(copy)
+    sibling = plane_dev((0, 1))
+
+    def chip_sums(acts, weights, firsts, ps, sib, sums, rs, sib_ss, sib_rs, ss, rs_rs):
+        halves = []
+        for d in (2, 1, 3, 0):
+            chip = (y + d) % 4
+            for n, first in enumerate(firsts):
+                at = pl.multiple_of(first + chip * (2 * HC), 2 * HC)
+                part = nn_dot(acts, weights[:, pl.ds(at, 2 * HC)])
+                ps[d, 0, :, n * HC : (n + 1) * HC] = part[:, :HC]
+                ps[d, 1, :, n * HC : (n + 1) * HC] = part[:, HC:]
+            copy = remote(ps.at[d, 1 - core], sib.at[d], sib_ss.at[d], sib_rs.at[d], sibling)
+            copy.start()
+            halves.append(copy)
+            pending.append(copy)
+        out = []
+        for k, d in enumerate((2, 1, 3)):
+            halves[k].wait_recv()
+            sums[k] = (ps[d, core] + sib[d]).astype(SUM_T)
+            copy = remote(sums.at[k], rs.at[k], ss.at[k], rs_rs.at[k], plane_dev((d, 0)))
+            copy.start()
+            out.append(copy)
+            pending.append(copy)
+        halves[3].wait_recv()
+        return out
+
+    def whole(ps, sib, rs):
+        total = ps[0, core] + sib[0]
+        for k in range(3):
+            total = total + rs[k].astype(F32)
+        return total
+
+    def gather_sends(ref, ss, rs):
+        out = []
+        for k, pair in enumerate(((2, 0), (1, 0), (3, 0), (0, 1))):
+            copy = remote(ref.at[me], ref.at[me], ss.at[k], rs.at[k], plane_dev(pair))
+            copy.start()
+            out.append(copy)
+            pending.append(copy)
+        return out
+
+    def gather_forwards(copies, ref, ss, rs):
+        out = [copies[3]]
+        for k, d in enumerate((2, 1, 3)):
+            copies[k].wait_recv()
+            source = ((y + 4 - d) % 4) * 2 + core
+            copy = remote(ref.at[source], ref.at[source], ss.at[4 + k], rs.at[4 + k], sibling)
+            copy.start()
+            out.append(copy)
+            pending.append(copy)
+        return out
+
+    in_rsa = chip_sums(r2_a[...].reshape(ROWS, SL), wgu, (0, FF), ps_a, sib_a, sum_a, rs_a,
+                       sba_ss, sba_rs, rsa_ss, rsa_rs)
 
     for copy in in_rsa:
         copy.wait_recv()
-    total = own_a[core]
-    for k in range(len(PAIRS)):
-        total = total + rs_a[k].astype(F32)
+    total = whole(ps_a, sib_a, rs_a)
     gate, up = total[:, :HC], total[:, HC:]
     h_a[me] = (gate * jax.nn.sigmoid(gate) * up).astype(BF)
-    in_aga = plane_sends(lambda pair: [(h_a.at[me], h_a.at[me], aga_ss, aga_rs)])
-
-    for copy in in_rsb:
-        copy.wait_recv()
-    dhid = own_b[core]
-    for k in range(len(PAIRS)):
-        dhid = dhid + rs_b[k].astype(F32)
-    held = r2_b[:, :, SL:].reshape(ROWS, 2 * HC).astype(F32)
-    gate, up = held[:, :HC], held[:, HC:]
-    sig = jax.nn.sigmoid(gate)
-    g_b[me, :, :HC] = (dhid * up * sig * (1.0 + gate * (1.0 - sig))).astype(BF)
-    g_b[me, :, HC:] = (dhid * gate * sig).astype(BF)
-    in_agb = plane_sends(lambda pair: [(g_b.at[me], g_b.at[me], agb_ss, agb_rs)])
+    in_aga = gather_sends(h_a, aga_ss, aga_rs)
+    in_aga = gather_forwards(in_aga, h_a, aga_ss, aga_rs)
+
+    for copy in in_2b:
+        copy.wait_recv()
+    early_relay(0)
+    in_rsb = chip_sums(r2_b[:, :, :SL].reshape(ROWS, SL), wd, (0,), ps_b, sib_b, sum_b, rs_b,
+                       sbb_ss, sbb_rs, rsb_ss, rsb_rs)
 
     for copy in in_aga:
         copy.wait_recv()
@@ -310,6 +375,17 @@
         eo_a[:, :, q : q + 128] = out.reshape(EXPERTS, ZROWS, 128)
     in_3a = depth_sends(eo_a, r3_a, rta_ss, rta_rs)
     r3_a[layer] = eo_a[layer]
+
+    for copy in in_rsb:
+        copy.wait_recv()
+    dhid = whole(ps_b, sib_b, rs_b)
+    held = r2_b[:, :, SL:].reshape(ROWS, 2 * HC).astype(F32)
+    gate, up = held[:, :HC], held[:, HC:]
+    sig = jax.nn.sigmoid(gate)
+    g_b[me, :, :HC] = (dhid * up * sig * (1.0 + gate * (1.0 - sig))).astype(BF)
+    g_b[me, :, HC:] = (dhid * gate * sig).astype(BF)
+    in_agb = gather_sends(g_b, agb_ss, agb_rs)
+    in_agb = gather_forwards(in_agb, g_b, agb_ss, agb_rs)
 
     for copy in in_agb:
         copy.wait_recv()
@@ -320,6 +396,7 @@
         eo_b[:, :, q : q + 128] = out.astype(BF).reshape(EXPERTS, ZROWS, 128)
     in_3b = depth_sends(eo_b, r3_b, rtb_ss, rtb_rs)
     r3_b[layer] = eo_b[layer]
+    early_relay(1)
 
     def last_sends(src, dst, ss, rs, sec):
         lane = pl.multiple_of(me * SL, SL)
@@ -345,17 +422,22 @@
     came = back(r3_a)
     for p in range(GROUP):
         s4_a[p] = (r1_a[p].astype(F32) + columns[p] * came[p]).astype(BF)
+
+    for copy in in_3b:
+        copy.wait_recv()
     last_sends(s4_a, rows_a, fa_ss, fa_rs, ahead)
-
-    for copy in in_3b:
-        copy.wait_recv()
     came = back(r3_b)
     for p in range(GROUP):
         s4_b[p] = (r1_b[p, :, :SL].astype(F32) + came[p]).astype(BF)
     last_sends(s4_b, rows_b, fb_ss, fb_rs, behind)
 
+    for b in (0, 1):
+        for i in range(3):
+            finals.append(early_copy(b, i, own_piece(b, i), sign[b]))
     for copy in finals:
         copy.wait_recv()
+    for cond, copy in guarded:
+        pl.when(cond)(copy.wait_send)
     for copy in pending:
         copy.wait_send()
 
@@ -373,16 +455,18 @@
         v((GROUP, SLOTS, SL), BF), v((GROUP, SLOTS, wide), BF),
         v((EXPERTS, ZROWS, SL), BF), v((EXPERTS, ZROWS, wide), BF),
         v((EXPERTS, ZROWS, SL), BF), v((EXPERTS, ZROWS, wide), BF),
-        v((4, 2, ROWS, 2 * HC), SUM_T), v((4, 2, ROWS, HC), SUM_T), v((2, ROWS, 2 * HC), F32), v((2, ROWS, HC), F32),
-        v((n, ROWS, 2 * HC), SUM_T), v((n, ROWS, HC), SUM_T),
+        v((4, 2, ROWS, 2 * HC), F32), v((4, 2, ROWS, HC), F32), v((4, ROWS, 2 * HC), F32), v((4, ROWS, HC), F32),
+        v((3, ROWS, 2 * HC), SUM_T), v((3, ROWS, HC), SUM_T), v((3, ROWS, 2 * HC), SUM_T), v((3, ROWS, HC), SUM_T),
         v((GROUP, ROWS, HC), BF), v((GROUP, ROWS, 2 * HC), BF),
         v((EXPERTS, ZROWS, SL), BF), v((EXPERTS, ZROWS, SL), BF),
         v((EXPERTS, ZROWS, SL), BF), v((EXPERTS, ZROWS, SL), BF),
         v((GROUP, SLOTS, SL), BF), v((GROUP, SLOTS, SL), BF),
+        v((PIECES[1][1], D), BF), v((PIECES[1][1], D), BF),
         dma((6,)),
     ]
-    for size in (n, n, n, 3, 3, n, n, n, n, 3, 3, GROUP, GROUP, 4):
-        scratch += [dma((size,)), dma((size,))]
+    for size in (n, n, n, 3, 3, 4, 4, 3, 3, n, n, 3, 3, GROUP, GROUP, (2, 4), 2):
+        shape = size if isinstance(size, tuple) else (size,)
+        scratch += [dma(shape), dma(shape)]
     return pl.pallas_call(
         kernel,
         out_shape=[

time: 217 us -> 163 us (0.75)
  the two profiles are of different devices: /device:TPU:197 before, /device:TPU:65 now
where the time goes in v2:
time: 163 us
  Pallas kernels  157 us (96%)
  matrix products  5.43 us (3%)
    pallas_call x1, Pallas kernels, relay_layer(): pl.pallas_call(kernel, out_shape=[jax.ShapeDtypeStruct((TOK, D), BF), jax...  157 us
    dot_general x2, matrix products, per_device(): jnp.einsum('rt,rd->td', perm, rows, preferred_element_type=F32).astype(BF)  5.43 us

profile of v2, /device:TPU:65, one launch (start us, length us, event | category | flops | bytes accessed | tf_op | source)
XLA Modules:
  0.0 162.9 jit_solution(3384129944618892186)
XLA Ops:
  0.6 156.8 %expert_relay.1 = (bf16[128,7168]{1,0:T(8,128)(2,1)}, bf16[128,7168]{1,0:T(8,128)(2,1)}, bf16[128,128]{1,0:T(8,128)(2,1)}, bf16[128,128]{1,0:T(8,128)(2,1)}) custom-call(s32[1,128]{1,0:T(1,128)} %bitcast.8, f32[1,128]{1,0:T(1,128)} %bitcast.9, s32[1,128]{1,0:T(1,128)} %bitcast.10, f32[1,128]{1,0:T(1,128)} %bitcast.11, bf16[128,7168]{1,0:T(8,128)(2,1)} %x_hbm.1, ...), custom_call_target="tpu_custom_call" | custom-call | tf_op jit(solution)/shard_map/expert_relay/pallas_call | solution.py:470
  157.4 0.0 copy-start
  157.4 0.0 copy-start.1
  157.4 3.5 %convolution_convert_fusion.1 = bf16[128,7168]{1,0:T(8,128)(2,1)} fusion(bf16[128,128]{1,0:T(8,128)(2,1)} %get-tuple-element.6, bf16[128,7168]{1,0:T(8,128)(2,1)} %get-tuple-element.7), kind=kOutput, calls=%fused_computation.1 | convolution fusion | flops 235798528 | bytes 3702784 | tf_op jit(solution)/shard_map/rt,rd->td/dot_general | solution.py:491
  161.0 0.0 copy-done
  161.0 0.0 copy-done.1
  161.0 1.9 %convolution_convert_fusion = bf16[128,7168]{1,0:T(8,128)(2,1)} fusion(bf16[128,128]{1,0:T(8,128)(2,1)S(1)} %copy-done.1, bf16[128,7168]{1,0:T(8,128)(2,1)S(1)} %copy-done), kind=kOutput, calls=%fused_computation | convolution fusion | flops 235798528 | bytes 3702784 | tf_op jit(solution)/shard_map/rt,rd->td/dot_general | solution.py:491
Async XLA Ops:
  157.4 3.6 %copy-start = (bf16[128,7168]{1,0:T(8,128)(2,1)S(1)}, bf16[128,7168]{1,0:T(8,128)(2,1)}, u32[]{:S(2)}) copy-start(bf16[128,7168]{1,0:T(8,128)(2,1)} %get-tuple-element.9) | copy-start | bytes 5505028
  157.4 3.6 %copy-start.1 = (bf16[128,128]{1,0:T(8,128)(2,1)S(1)}, bf16[128,128]{1,0:T(8,128)(2,1)}, u32[]{:S(2)}) copy-start(bf16[128,128]{1,0:T(8,128)(2,1)} %get-tuple-element.8) | copy-start | bytes 98308

commit v3 on v2

--- a/solution.py
+++ b/solution.py
@@ -23,7 +23,8 @@
 BF = jnp.bfloat16
 F32 = jnp.float32
 SUM_T = jnp.bfloat16
-PIECES = [(0, 16), (16, 32), (48, 32)]
+CUTS = [(0, 384), (384, 896)]
+PIECES = [(0, 16), (16, 16), (32, 32), (64, 16)]
 PAIRS = [(2, 0), (2, 1), (1, 0), (1, 1), (3, 0), (3, 1), (0, 1)]
 
 
@@ -87,7 +88,7 @@
     pk_a, pk_b, early_a, early_b,
     r1_a, r1_b, s2_a, s2_b, r2_a, r2_b,
     ps_a, ps_b, sib_a, sib_b, sum_a, sum_b, rs_a, rs_b,
-    h_a, g_b, eo_a, eo_b, r3_a, r3_b, s4_a, s4_b, rl_a, rl_b,
+    h_a, g_b, eo_a, eo_b, r3_a, r3_b, s4_a, s4_b, near_a, near_b, far_a, far_b,
     load_sem,
     sc_ss, sc_rs, d1a_ss, d1a_rs, d1b_ss, d1b_rs, d2a_ss, d2a_rs, d2b_ss, d2b_rs,
     sba_ss, sba_rs, sbb_ss, sbb_rs, rsa_ss, rsa_rs, rsb_ss, rsb_rs, aga_ss, aga_rs, agb_ss, agb_rs,
@@ -164,7 +165,8 @@
 
     rows_of = {0: rows_a, 1: rows_b}
     early_of = {0: early_a, 1: early_b}
-    relay_of = {0: rl_a, 1: rl_b}
+    relay_of = {(0, 2): near_a, (0, 3): far_a, (1, 2): near_b, (1, 3): far_b}
+    relay_at = {(0, 2): x == 2, (0, 3): x == 1, (1, 2): x == 1, (1, 3): x == 2}
     sign = {0: 1, 1: -1}
 
     def early_copy(b, i, src, step):
@@ -180,30 +182,34 @@
         copy = early_copy(b, 0, own_piece(b, 0), sign[b])
         copy.start()
         pending.append(copy)
-        for i in (1, 2):
-            copy = remote(own_piece(b, i), relay_of[b], e_ss.at[b, i], rl_rs.at[b],
-                          (sec_at(-i * sign[b]), place))
+        for i in (2, 3):
+            copy = remote(own_piece(b, i), relay_of[b, i], e_ss.at[b, i], rl_rs.at[b, i],
+                          (sec_at((1 - i) * sign[b]), place))
             when_send(edges[b], copy)
 
     def early_direct():
         for b in (0, 1):
-            for i in (1, 2):
+            for i in (1, 2, 3):
                 when_send(jnp.logical_not(edges[b]), early_copy(b, i, own_piece(b, i), sign[b]))
         for b, (src, dst) in enumerate(((pm_a, perm_a), (pm_b, perm_b))):
-            copy = remote(src, dst, e_ss.at[b, 3], e_rs.at[b, 3], (sec_at(sign[b]), place))
+            copy = remote(src, dst, e_ss.at[b, 4], e_rs.at[b, 4], (sec_at(sign[b]), place))
             copy.start()
             finals.append(copy)
             pending.append(copy)
 
-    def early_relay(b):
-        for i in (1, 2):
-            there = x == (3 - i if b == 0 else i)
-            copy = remote(relay_of[b], rows_of[b].at[pl.ds(SLOTS + PIECES[i][0], PIECES[i][1]), :],
-                          rl_ss.at[b], e_rs.at[b, i], (sec_at((i + 1) * sign[b]), place))
+    def early_border():
+        for b in (0, 1):
+            when_send(edges[b], early_copy(b, 1, own_piece(b, 1), sign[b]))
+
+    def early_relay(i):
+        for b in (0, 1):
+            buf, there = relay_of[b, i], relay_at[b, i]
+            copy = remote(buf, rows_of[b].at[pl.ds(SLOTS + PIECES[i][0], PIECES[i][1]), :],
+                          rl_ss.at[b, i], e_rs.at[b, i], (sec_at(i * sign[b]), place))
 
             @pl.when(there)
             def _():
-                remote(relay_of[b], relay_of[b], rl_ss.at[b], rl_rs.at[b], (sec_at(1), place)).wait_recv()
+                remote(buf, buf, rl_ss.at[b, i], rl_rs.at[b, i], (sec_at(1), place)).wait_recv()
                 copy.start()
 
             guarded.append((there, copy))
@@ -263,10 +269,10 @@
             for p in range(GROUP)
         ]
 
-    def depth_sends(src, dst, ss, rs):
+    def depth_sends(src, dst, ss, rs, cols=slice(None)):
         out = []
         for i, step in enumerate((2, 1, 3)):
-            copy = remote(src.at[depth(step)], dst.at[layer], ss.at[i], rs.at[i], depth_dev(step))
+            copy = remote(src.at[depth(step), :, cols], dst.at[layer, :, cols], ss.at[i], rs.at[i], depth_dev(step))
             copy.start()
             out.append(copy)
             pending.append(copy)
@@ -360,20 +366,24 @@
     h_a[me] = (gate * jax.nn.sigmoid(gate) * up).astype(BF)
     in_aga = gather_sends(h_a, aga_ss, aga_rs)
     in_aga = gather_forwards(in_aga, h_a, aga_ss, aga_rs)
+    early_relay(3)
+    early_border()
 
     for copy in in_2b:
         copy.wait_recv()
-    early_relay(0)
     in_rsb = chip_sums(r2_b[:, :, :SL].reshape(ROWS, SL), wd, (0,), ps_b, sib_b, sum_b, rs_b,
                        sbb_ss, sbb_rs, rsb_ss, rsb_rs)
 
     for copy in in_aga:
         copy.wait_recv()
     hidden = jnp.concatenate([h_a[p] for p in range(GROUP)], axis=1)
-    for q in range(0, SL, 128):
-        out = nt_dot(hidden, wd[q : q + 128, :]).astype(BF)
-        eo_a[:, :, q : q + 128] = out.reshape(EXPERTS, ZROWS, 128)
-    in_3a = depth_sends(eo_a, r3_a, rta_ss, rta_rs)
+    in_3a = []
+    for n, (first, last) in enumerate(CUTS):
+        for q in range(first, last, 128):
+            out = nt_dot(hidden, wd[q : q + 128, :]).astype(BF)
+            eo_a[:, :, q : q + 128] = out.reshape(EXPERTS, ZROWS, 128)
+        part = pl.ds(first, last - first)
+        in_3a += depth_sends(eo_a, r3_a, rta_ss.at[n], rta_rs.at[n], part)
     r3_a[layer] = eo_a[layer]
 
     for copy in in_rsb:
@@ -391,12 +401,14 @@
         copy.wait_recv()
     left = jnp.concatenate([g_b[p, :, :HC] for p in range(GROUP)], axis=1)
     right = jnp.concatenate([g_b[p, :, HC:] for p in range(GROUP)], axis=1)
-    for q in range(0, SL, 128):
-        out = nt_dot(left, wgu[q : q + 128, :FF]) + nt_dot(right, wgu[q : q + 128, FF:])
-        eo_b[:, :, q : q + 128] = out.astype(BF).reshape(EXPERTS, ZROWS, 128)
-    in_3b = depth_sends(eo_b, r3_b, rtb_ss, rtb_rs)
+    in_3b = []
+    for n, (first, last) in enumerate(CUTS):
+        for q in range(first, last, 128):
+            out = nt_dot(left, wgu[q : q + 128, :FF]) + nt_dot(right, wgu[q : q + 128, FF:])
+            eo_b[:, :, q : q + 128] = out.astype(BF).reshape(EXPERTS, ZROWS, 128)
+        part = pl.ds(first, last - first)
+        in_3b += depth_sends(eo_b, r3_b, rtb_ss.at[n], rtb_rs.at[n], part)
     r3_b[layer] = eo_b[layer]
-    early_relay(1)
 
     def last_sends(src, dst, ss, rs, sec):
         lane = pl.multiple_of(me * SL, SL)
@@ -426,13 +438,14 @@
     for copy in in_3b:
         copy.wait_recv()
     last_sends(s4_a, rows_a, fa_ss, fa_rs, ahead)
+    early_relay(2)
     came = back(r3_b)
     for p in range(GROUP):
         s4_b[p] = (r1_b[p, :, :SL].astype(F32) + came[p]).astype(BF)
     last_sends(s4_b, rows_b, fb_ss, fb_rs, behind)
 
     for b in (0, 1):
-        for i in range(3):
+        for i in range(4):
             finals.append(early_copy(b, i, own_piece(b, i), sign[b]))
     for copy in finals:
         copy.wait_recv()
@@ -461,10 +474,10 @@
         v((EXPERTS, ZROWS, SL), BF), v((EXPERTS, ZROWS, SL), BF),
         v((EXPERTS, ZROWS, SL), BF), v((EXPERTS, ZROWS, SL), BF),
         v((GROUP, SLOTS, SL), BF), v((GROUP, SLOTS, SL), BF),
-        v((PIECES[1][1], D), BF), v((PIECES[1][1], D), BF),
+        v((PIECES[2][1], D), BF), v((PIECES[2][1], D), BF), v((PIECES[3][1], D), BF), v((PIECES[3][1], D), BF),
         dma((6,)),
     ]
-    for size in (n, n, n, 3, 3, 4, 4, 3, 3, n, n, 3, 3, GROUP, GROUP, (2, 4), 2):
+    for size in (n, n, n, 3, 3, 4, 4, 3, 3, n, n, (2, 3), (2, 3), GROUP, GROUP, (2, 5), (2, 4)):
         shape = size if isinstance(size, tuple) else (size,)
         scratch += [dma(shape), dma(shape)]
     return pl.pallas_call(

time: 163 us -> 155 us (0.951)
  Pallas kernels: 157 us -> 149 us
    pallas_call x1, Pallas kernels: 157 us -> 149 us  [relay_layer(): pl.pallas_call(kernel, out_shape=[jax.ShapeDtypeStruct((TOK, D), BF), jax...]
where the time goes in v3:
time: 155 us
  Pallas kernels  149 us (96%)
  matrix products  5.44 us (4%)
    pallas_call x1, Pallas kernels, relay_layer(): pl.pallas_call(kernel, out_shape=[jax.ShapeDtypeStruct((TOK, D), BF), jax...  149 us
    dot_general x2, matrix products, per_device(): jnp.einsum('rt,rd->td', perm, rows, preferred_element_type=F32).astype(BF)  5.44 us

profile of v3, /device:TPU:65, one launch (start us, length us, event | category | flops | bytes accessed | tf_op | source)
XLA Modules:
  0.0 154.7 jit_solution(4192949177020777570)
XLA Ops:
  0.6 148.6 %expert_relay.1 = (bf16[128,7168]{1,0:T(8,128)(2,1)}, bf16[128,7168]{1,0:T(8,128)(2,1)}, bf16[128,128]{1,0:T(8,128)(2,1)}, bf16[128,128]{1,0:T(8,128)(2,1)}) custom-call(s32[1,128]{1,0:T(1,128)} %bitcast.8, f32[1,128]{1,0:T(1,128)} %bitcast.9, s32[1,128]{1,0:T(1,128)} %bitcast.10, f32[1,128]{1,0:T(1,128)} %bitcast.11, bf16[128,7168]{1,0:T(8,128)(2,1)} %x_hbm.1, ...), custom_call_target="tpu_custom_call" | custom-call | tf_op jit(solution)/shard_map/expert_relay/pallas_call | solution.py:483
  149.2 0.0 copy-start
  149.2 0.0 copy-start.1
  149.2 3.5 %convolution_convert_fusion.1 = bf16[128,7168]{1,0:T(8,128)(2,1)} fusion(bf16[128,128]{1,0:T(8,128)(2,1)} %get-tuple-element.6, bf16[128,7168]{1,0:T(8,128)(2,1)} %get-tuple-element.7), kind=kOutput, calls=%fused_computation.1 | convolution fusion | flops 235798528 | bytes 3702784 | tf_op jit(solution)/shard_map/rt,rd->td/dot_general | solution.py:504
  152.8 0.0 copy-done
  152.8 0.0 copy-done.1
  152.8 1.9 %convolution_convert_fusion = bf16[128,7168]{1,0:T(8,128)(2,1)} fusion(bf16[128,128]{1,0:T(8,128)(2,1)S(1)} %copy-done.1, bf16[128,7168]{1,0:T(8,128)(2,1)S(1)} %copy-done), kind=kOutput, calls=%fused_computation | convolution fusion | flops 235798528 | bytes 3702784 | tf_op jit(solution)/shard_map/rt,rd->td/dot_general | solution.py:504
Async XLA Ops:
  149.2 3.6 %copy-start = (bf16[128,7168]{1,0:T(8,128)(2,1)S(1)}, bf16[128,7168]{1,0:T(8,128)(2,1)}, u32[]{:S(2)}) copy-start(bf16[128,7168]{1,0:T(8,128)(2,1)} %get-tuple-element.9) | copy-start | bytes 5505028
  149.2 3.6 %copy-start.1 = (bf16[128,128]{1,0:T(8,128)(2,1)S(1)}, bf16[128,128]{1,0:T(8,128)(2,1)}, u32[]{:S(2)}) copy-start(bf16[128,128]{1,0:T(8,128)(2,1)} %get-tuple-element.8) | copy-start | bytes 98308

commit v4 on v3

--- a/solution.py
+++ b/solution.py
@@ -396,6 +396,7 @@
     g_b[me, :, HC:] = (dhid * gate * sig).astype(BF)
     in_agb = gather_sends(g_b, agb_ss, agb_rs)
     in_agb = gather_forwards(in_agb, g_b, agb_ss, agb_rs)
+    early_relay(2)
 
     for copy in in_agb:
         copy.wait_recv()
@@ -438,7 +439,6 @@
     for copy in in_3b:
         copy.wait_recv()
     last_sends(s4_a, rows_a, fa_ss, fa_rs, ahead)
-    early_relay(2)
     came = back(r3_b)
     for p in range(GROUP):
         s4_b[p] = (r1_b[p, :, :SL].astype(F32) + came[p]).astype(BF)

time: 155 us -> 153 us (0.987)
  Pallas kernels: 149 us -> 147 us
    pallas_call x1, Pallas kernels: 149 us -> 147 us  [relay_layer(): pl.pallas_call(kernel, out_shape=[jax.ShapeDtypeStruct((TOK, D), BF), jax...]
where the time goes in v4:
time: 153 us
  Pallas kernels  147 us (96%)
  matrix products  5.45 us (4%)
    pallas_call x1, Pallas kernels, relay_layer(): pl.pallas_call(kernel, out_shape=[jax.ShapeDtypeStruct((TOK, D), BF), jax...  147 us
    dot_general x2, matrix products, per_device(): jnp.einsum('rt,rd->td', perm, rows, preferred_element_type=F32).astype(BF)  5.45 us

profile of v4, /device:TPU:65, one launch (start us, length us, event | category | flops | bytes accessed | tf_op | source)
XLA Modules:
  0.0 153.0 jit_solution(13526870573449845952)
XLA Ops:
  0.6 146.9 %expert_relay.1 = (bf16[128,7168]{1,0:T(8,128)(2,1)}, bf16[128,7168]{1,0:T(8,128)(2,1)}, bf16[128,128]{1,0:T(8,128)(2,1)}, bf16[128,128]{1,0:T(8,128)(2,1)}) custom-call(s32[1,128]{1,0:T(1,128)} %bitcast.8, f32[1,128]{1,0:T(1,128)} %bitcast.9, s32[1,128]{1,0:T(1,128)} %bitcast.10, f32[1,128]{1,0:T(1,128)} %bitcast.11, bf16[128,7168]{1,0:T(8,128)(2,1)} %x_hbm.1, ...), custom_call_target="tpu_custom_call" | custom-call | tf_op jit(solution)/shard_map/expert_relay/pallas_call | solution.py:483
  147.5 0.0 copy-start
  147.5 0.0 copy-start.1
  147.5 3.6 %convolution_convert_fusion.1 = bf16[128,7168]{1,0:T(8,128)(2,1)} fusion(bf16[128,128]{1,0:T(8,128)(2,1)} %get-tuple-element.6, bf16[128,7168]{1,0:T(8,128)(2,1)} %get-tuple-element.7), kind=kOutput, calls=%fused_computation.1 | convolution fusion | flops 235798528 | bytes 3702784 | tf_op jit(solution)/shard_map/rt,rd->td/dot_general | solution.py:504
  151.1 0.0 copy-done
  151.1 0.0 copy-done.1
  151.1 1.9 %convolution_convert_fusion = bf16[128,7168]{1,0:T(8,128)(2,1)} fusion(bf16[128,128]{1,0:T(8,128)(2,1)S(1)} %copy-done.1, bf16[128,7168]{1,0:T(8,128)(2,1)S(1)} %copy-done), kind=kOutput, calls=%fused_computation | convolution fusion | flops 235798528 | bytes 3702784 | tf_op jit(solution)/shard_map/rt,rd->td/dot_general | solution.py:504
Async XLA Ops:
  147.5 3.6 %copy-start = (bf16[128,7168]{1,0:T(8,128)(2,1)S(1)}, bf16[128,7168]{1,0:T(8,128)(2,1)}, u32[]{:S(2)}) copy-start(bf16[128,7168]{1,0:T(8,128)(2,1)} %get-tuple-element.9) | copy-start | bytes 5505028
  147.5 3.6 %copy-start.1 = (bf16[128,128]{1,0:T(8,128)(2,1)S(1)}, bf16[128,128]{1,0:T(8,128)(2,1)}, u32[]{:S(2)}) copy-start(bf16[128,128]{1,0:T(8,128)(2,1)} %get-tuple-element.8) | copy-start | bytes 98308

commit v5 on v4

--- a/solution.py
+++ b/solution.py
@@ -411,7 +411,7 @@
         in_3b += depth_sends(eo_b, r3_b, rtb_ss.at[n], rtb_rs.at[n], part)
     r3_b[layer] = eo_b[layer]
 
-    def last_sends(src, dst, ss, rs, sec):
+    def last_sends(src, dst, ss, rs, sec, cond=None):
         lane = pl.multiple_of(me * SL, SL)
         for p in range(GROUP):
             other = (me + p) % GROUP
@@ -419,9 +419,13 @@
                 src.at[other], dst.at[pl.ds(0, SLOTS), pl.ds(lane, SL)],
                 ss.at[p], rs.at[p], (sec, layer * GROUP + other),
             )
-            copy.start()
-            finals.append(copy)
-            pending.append(copy)
+            if cond is None:
+                copy.start()
+            else:
+                pl.when(cond)(copy.start)
+            if cond is not edges[0]:
+                finals.append(copy)
+                pending.append(copy)
 
     def back(ref):
         return lax.dot_general(
@@ -436,9 +440,11 @@
     for p in range(GROUP):
         s4_a[p] = (r1_a[p].astype(F32) + columns[p] * came[p]).astype(BF)
 
+    last_sends(s4_a, rows_a, fa_ss, fa_rs, ahead, jnp.logical_not(edges[0]))
+
     for copy in in_3b:
         copy.wait_recv()
-    last_sends(s4_a, rows_a, fa_ss, fa_rs, ahead)
+    last_sends(s4_a, rows_a, fa_ss, fa_rs, ahead, edges[0])
     came = back(r3_b)
     for p in range(GROUP):
         s4_b[p] = (r1_b[p, :, :SL].astype(F32) + came[p]).astype(BF)
@@ -496,13 +502,33 @@
     )(routes_a, scale_a, routes_b, scale_b, x, cot, saved, wgu, wd, jnp.asarray(regroup_matrix(), BF))
 
 
+def token_order_kernel(perm_a, rows_a, perm_b, rows_b, out_a, out_b):
+    for perm, rows, out in ((perm_a, rows_a, out_a), (perm_b, rows_b, out_b)):
+        out[...] = lax.dot_general(
+            perm[...], rows[...], (((0,), (0,)), ((), ())), preferred_element_type=F32
+        ).astype(BF)
+
+
+def token_order(perm_a, rows_a, perm_b, rows_b):
+    tile = 1792
+    square = pl.BlockSpec((TOK, TOK), lambda i: (0, 0))
+    wide = pl.BlockSpec((TOK, tile), lambda i: (0, i))
+    return pl.pallas_call(
+        token_order_kernel,
+        grid=(D // tile,),
+        out_shape=[jax.ShapeDtypeStruct((TOK, D), BF)] * 2,
+        in_specs=[square, wide, square, wide],
+        out_specs=[wide, wide],
+        name="token_order",
+    )(perm_a, rows_a, perm_b, rows_b)
+
+
 def per_device(x_a, routes_a, scale_a, cotangent_b, routes_b, scale_b, saved_b, w_gate_up, w_down_t):
     rows_a, rows_b, perm_a, perm_b = relay_layer(
         routes_a.reshape(1, TOK), scale_a.reshape(1, TOK), routes_b.reshape(1, TOK), scale_b.reshape(1, TOK),
         x_a, cotangent_b, saved_b, w_gate_up, w_down_t,
     )
-    put = lambda perm, rows: jnp.einsum("rt,rd->td", perm, rows, preferred_element_type=F32).astype(BF)
-    return put(perm_a, rows_a), put(perm_b, rows_b)
+    return token_order(perm_a, rows_a, perm_b, rows_b)
 
 
 def solution(mesh):

time: 153 us -> 153 us (level)
  matrix products: 5.45 us -> 0 us
  Pallas kernels: 147 us -> 152 us
    dot_general x2 -> x0, matrix products: 5.45 us -> none  [per_device(): jnp.einsum('rt,rd->td', perm, rows, preferred_element_type=F32).astype(BF)]
    pallas_call x0 -> x1, Pallas kernels: none -> 5.02 us  [token_order(): pl.pallas_call(token_order_kernel, grid=(D // tile,), out_shape=[jax.Shap...]
where the time goes in v5:
time: 153 us
  Pallas kernels  152 us (99%)
    pallas_call x1, Pallas kernels, relay_layer(): pl.pallas_call(kernel, out_shape=[jax.ShapeDtypeStruct((TOK, D), BF), jax...  147 us
    pallas_call x1, Pallas kernels, token_order(): pl.pallas_call(token_order_kernel, grid=(D // tile,), out_shape=[jax.Shap...  5.02 us

profile of v5, /device:TPU:65, one launch (start us, length us, event | category | flops | bytes accessed | tf_op | source)
XLA Modules:
  0.0 152.5 jit_solution(8811214817292651480)
XLA Ops:
  0.6 146.9 %expert_relay.1 = (bf16[128,7168]{1,0:T(8,128)(2,1)}, bf16[128,7168]{1,0:T(8,128)(2,1)}, bf16[128,128]{1,0:T(8,128)(2,1)}, bf16[128,128]{1,0:T(8,128)(2,1)}) custom-call(s32[1,128]{1,0:T(1,128)} %bitcast.4, f32[1,128]{1,0:T(1,128)} %bitcast.5, s32[1,128]{1,0:T(1,128)} %bitcast.6, f32[1,128]{1,0:T(1,128)} %bitcast.7, bf16[128,7168]{1,0:T(8,128)(2,1)} %x_hbm.1, ...), custom_call_target="tpu_custom_call" | custom-call | tf_op jit(solution)/shard_map/expert_relay/pallas_call | solution.py:489
  147.5 5.0 %token_order.1 = (bf16[128,7168]{1,0:T(8,128)(2,1)}, bf16[128,7168]{1,0:T(8,128)(2,1)}) custom-call(bf16[128,128]{1,0:T(8,128)(2,1)} %get-tuple-element.6.perm_a, bf16[128,7168]{1,0:T(8,128)(2,1)} %get-tuple-element.7.rows_a, bf16[128,128]{1,0:T(8,128)(2,1)} %get-tuple-element.8.perm_b, bf16[128,7168]{1,0:T(8,128)(2,1)} %get-tuple-element.9.rows_b), custom_call_target="tpu_custom_call" | custom-call | tf_op jit(solution)/shard_map/token_order/pallas_call | solution.py:516
